TPU v7x, 32 devices: a whole 2x2x4 slice. The times are simulated.
32 devices in a mesh: group: 2 (over y), attn: 4 (over z), expert: 4 (over x, core).
Axes of the slice: x: 2, y: 2, z: 4, core: 2. Of those that a mesh axis runs over, the one named last changes fastest.
Arguments:
- queries: bfloat16 [1024, 5120], P(('group', 'attn'), 'expert'), parts along dimension 0, may hold values from -30 to 30
- kv_cache: bfloat16 [2, 1024, 64, 1024], P(None, ('group', 'attn'), None, 'expert'), parts along dimension 1, may hold values from -30 to 30
- lengths: int32 [1024], P(('group', 'attn')), parts along dimension 0, may hold values from 2 to 64, as said below
- out_weight: bfloat16 [5120, 5120], P('expert', 'attn'), may hold values from -0.625 to 0.625
- residual: bfloat16 [1024, 5120], P(('group', 'expert'), 'attn'), parts along dimension 0, may hold values from -6 to 6
- norm_gain: bfloat16 [5120], P('attn'), may hold values from 0.099609375 to 1.8984375
- route_logit: float32 [1024], P(('group', 'expert')), parts along dimension 0, may hold values from -6 to 6
- routes: int32 [1024, 1], P(('group', 'expert')), parts along dimension 0, may hold values from 0 to 3; in each aligned block of 128 rows (0 to 127, 128 to 255, ...) at most 32 rows name the same one
- w_gate_up: bfloat16 [4, 2, 5120, 4096], P('expert', None, None, 'attn'), may hold values from -0.078125 to 0.078125
- w_down: bfloat16 [4, 4096, 5120], P('expert', None, 'attn'), may hold values from -0.09375 to 0.09375
Outputs:
- mixed: bfloat16 [1024, 5120], P(('group', 'expert'), 'attn'), parts along dimension 0
There are 2 independent parts, one for each index of `group`. A program takes and returns all parts, laid end to end along the dimension named above; an argument that names none is the same for every part. Nothing has to cross between parts.
Inputs may be any that keep to these rules, and one draw needn't show every extreme that they name: `lengths`: request 0 has all 64 slots live. `routes`: within each aligned block of 128 requests no expert is named by more than 32 requests.
All inputs are finite; a program needn't handle non-finite values.
Results may differ from a plain program's by a relative error of at most 0.0049.
The roundings to bfloat16 on the way count: a program that leaves them out, or rounds other values in their place, can miss the bound.
Values may be sent and summed in bfloat16 or wider, within the bound.
A program may use at most 128 MiB of HBM per device.

v0:
```python
import math

import jax
import jax.numpy as jnp
from jax import lax
from jax.sharding import PartitionSpec as P

D = 5120
HEADS = 40
KV_HEADS = 8
HD = 128


def per_device(
    queries,
    kv_cache,
    lengths,
    out_weight,
    residual,
    norm_gain,
    route_logit,
    routes,
    w_gate_up,
    w_down,
):
    group_size = HEADS // KV_HEADS
    rows_dev = queries.shape[0]
    cache_span = kv_cache.shape[2]
    kv_dev = kv_cache.shape[3] // HD
    query_heads = queries.reshape(rows_dev, kv_dev, group_size, HD)
    key_heads = kv_cache[0].reshape(rows_dev, cache_span, kv_dev, HD)
    value_heads = kv_cache[1].reshape(rows_dev, cache_span, kv_dev, HD)
    scores = jnp.einsum(
        "rkgd,rlkd->rkgl", query_heads, key_heads, preferred_element_type=jnp.float32
    ) * (1.0 / math.sqrt(HD))
    live_mask = lax.broadcasted_iota(jnp.int32, (rows_dev, cache_span), 1) < lengths[:, None]
    scores = jnp.where(live_mask[:, None, None, :], scores, -jnp.inf)
    row_peak = jnp.max(scores, axis=-1, keepdims=True)
    expsum = jnp.exp(scores - row_peak)
    probs = (expsum / jnp.sum(expsum, axis=-1, keepdims=True)).astype(jnp.bfloat16)
    heads_out = jnp.einsum(
        "rkgl,rlkd->rkgd", probs, value_heads, preferred_element_type=jnp.float32
    )
    heads_out = heads_out.astype(jnp.bfloat16).reshape(rows_dev, kv_dev * group_size * HD)
    gathered = lax.all_gather(heads_out, "attn", axis=0, tiled=True)
    projected = lax.psum_scatter(
        jnp.dot(gathered, out_weight, preferred_element_type=jnp.float32),
        "expert",
        scatter_dimension=0,
        tiled=True,
    )
    hidden_state = residual.astype(jnp.float32) + projected
    total_sq = lax.psum(jnp.sum(hidden_state * hidden_state, axis=1), "attn")
    normed = (
        hidden_state * lax.rsqrt(total_sq[:, None] / D + 1e-05) * norm_gain.astype(jnp.float32)
    ).astype(jnp.bfloat16)
    moe_rows = normed.shape[0]
    experts = lax.axis_size("expert")
    capacity = moe_rows // 4
    slot_count = experts * capacity
    chosen = routes[:, 0]
    onehot = (chosen[:, None] == lax.broadcasted_iota(jnp.int32, (moe_rows, experts), 1)).astype(
        jnp.int32
    )
    slot_rank = jnp.sum((jnp.cumsum(onehot, axis=0) - onehot) * onehot, axis=1)
    slot_index = chosen * capacity + slot_rank
    placing = (
        slot_index[None, :] == lax.broadcasted_iota(jnp.int32, (slot_count, moe_rows), 0)
    ).astype(jnp.bfloat16)
    gate_w = w_gate_up[0, 0]
    up_w = w_gate_up[0, 1]
    down_w = w_down[0]
    outgoing = jnp.dot(placing, normed, preferred_element_type=jnp.float32).astype(jnp.bfloat16)
    arrived = lax.all_to_all(
        outgoing.reshape(experts, capacity, -1), "expert", split_axis=0, concat_axis=0, tiled=True
    )
    arrived = arrived.reshape(slot_count, -1)
    block_piece = lax.all_gather(arrived, "attn", axis=1, tiled=True)
    gate_acc = jnp.dot(block_piece, gate_w, preferred_element_type=jnp.float32)
    up_acc = jnp.dot(block_piece, up_w, preferred_element_type=jnp.float32)
    hidden_units = (jax.nn.silu(gate_acc) * up_acc).astype(jnp.bfloat16)
    expert_out = jnp.dot(
        lax.all_gather(hidden_units, "attn", axis=1, tiled=True),
        down_w,
        preferred_element_type=jnp.float32,
    ).astype(jnp.bfloat16)
    returned_rows = lax.all_to_all(
        expert_out.reshape(experts, capacity, -1), "expert", split_axis=0, concat_axis=0, tiled=True
    )
    returned_rows = returned_rows.reshape(slot_count, -1)
    combined = lax.dot_general(
        placing, returned_rows, (((0,), (0,)), ((), ())), preferred_element_type=jnp.float32
    )
    gate_prob = jax.nn.sigmoid(route_logit)[:, None]
    return (hidden_state + gate_prob * combined).astype(jnp.bfloat16)


def solution(mesh):
    return jax.shard_map(
        per_device,
        mesh=mesh,
        in_specs=(
            P(("group", "attn"), "expert"),
            P(None, ("group", "attn"), None, "expert"),
            P(("group", "attn")),
            P("expert", "attn"),
            P(("group", "expert"), "attn"),
            P("attn"),
            P(("group", "expert")),
            P(("group", "expert"), None),
            P("expert", None, None, "attn"),
            P("expert", None, "attn"),
        ),
        out_specs=P(("group", "expert"), "attn"),
        check_vma=False,
    )
```

profile of v0, /device:TPU:0, one launch (start us, length us, event | category | flops | bytes accessed | tf_op | source)
XLA Modules:
  0.0 251.0 jit_solution(13859708820870714403)
XLA Ops:
  6.5 6.2 %fusion.29 = (bf16[1,128,64,256]{3,2,1,0:T(8,128)(2,1)}, bf16[1,128,64,256]{3,2,1,0:T(8,128)(2,1)}) fusion(bf16[2,128,64,256]{3,2,1,0:T(8,128)(2,1)} %param.11), kind=kLoop, calls=%fused_computation.38 | loop fusion | bytes 16777216 | tf_op jit(solution)/shard_map/slice | solution.py:31
  12.7 6.9 %copy.18 = bf16[1,128,64,256]{1,3,2,0:T(8,128)(2,1)} copy(bf16[1,128,64,256]{3,2,1,0:T(8,128)(2,1)} %get-tuple-element.5) | data formatting | bytes 8388608
  19.6 6.6 %copy.14 = bf16[128,64,2,128]{3,1,2,0:T(8,128)(2,1)} copy(bf16[128,64,2,128]{0,3,2,1:T(8,128)(2,1)} %bitcast.34) | data formatting | bytes 8388608 | tf_op jit(solution)/shard_map/reshape;squeeze | solution.py:31
  26.2 1.9 copy.11
  28.1 2.2 copy.13
  30.3 6.9 %copy.19 = bf16[1,128,64,256]{1,3,2,0:T(8,128)(2,1)} copy(bf16[1,128,64,256]{3,2,1,0:T(8,128)(2,1)} %get-tuple-element.6) | data formatting | bytes 8388608
  37.2 6.6 %copy.16 = bf16[128,64,2,128]{3,1,2,0:T(8,128)(2,1)} copy(bf16[128,64,2,128]{0,3,2,1:T(8,128)(2,1)} %bitcast.35) | data formatting | bytes 8388608 | tf_op jit(solution)/shard_map/reshape;squeeze | solution.py:32
  43.8 5.9 %fusion.30 = (f32[128,2,5]{2,1,0:T(2,128)S(1)}, f32[128,2,5,64]{3,2,1,0:T(8,128)}) fusion(bf16[128,2,5,128]{3,2,1,0:T(8,128)(2,1)} %copy.13, bf16[128,64,2,128]{3,1,2,0:T(8,128)(2,1)} %copy.14, pred[128,64]{1,0:T(8,128)(4,1)S(1)} %iota_compare_fusion.4), kind=kOutput, calls=%fused_computation.39 | convolution fusion | flops 21299264 | bytes 4862976 | tf_op jit(solution)/shard_map/sub | solution.py:39
  49.7 4.6 %convolution_convert_fusion.1 = bf16[128,2,5,128]{3,2,1,0:T(8,128)(2,1)} fusion(bf16[128,64,2,128]{3,1,2,0:T(8,128)(2,1)} %copy.16, f32[128,2,5,64]{3,2,1,0:T(8,128)} %get-tuple-element.8, f32[128,2,5]{2,1,0:T(2,128)S(1)} %get-tuple-element.7), kind=kOutput, calls=%fused_computation.18 | convolution fusion | flops 21299200 | bytes 4854784 | tf_op jit(solution)/shard_map/rkgl,rlkd->rkgd/dot_general | solution.py:41
  54.2 2.1 copy.17
  56.4 36.2 %all-gather.4.cloned.1.call-done = bf16[512,1280]{0,1:T(8,128)(2,1)} async-done(((bf16[128,1280]{0,1:T(8,128)(2,1)}), bf16[512,1280]{0,1:T(8,128)(2,1)}) %all-gather.4.cloned.1.call-update) | async-done | bytes 1310736 | tf_op jit(solution)/shard_map/all_gather | solution.py:45
  92.6 4.7 %fusion.31 = f32[512,1280]{1,0:T(8,128)} fusion(bf16[512,1280]{0,1:T(8,128)(2,1)} %all-gather.4.cloned.1.call-done, bf16[1280,1280]{1,0:T(8,128)(2,1)S(1)} %copy-done), kind=kOutput, calls=%fused_computation.40 | convolution fusion | flops 1677721600 | bytes 7208960 | tf_op jit(solution)/shard_map/dot_general | solution.py:47
  97.9 32.8 %reduce-scatter.2.cloned.1.call-done = f32[128,1280]{1,0:T(8,128)} async-done(((f32[512,1280]{1,0:T(8,128)}), f32[128,1280]{1,0:T(8,128)}) %reduce-scatter.2.cloned.1.call-update) | async-done | bytes 655376 | tf_op jit(solution)/shard_map/reduce_scatter | solution.py:46
  132.1 11.7 %psum.7 = f32[128]{0:T(128)S(1)} all-reduce(f32[128]{0:T(128)S(1)} %multiply_reduce_fusion), channel_id=1, replica_groups=mesh['group'=2,'attn'=4,'expert'=4] {'attn'}, use_global_device_ids=true, to_apply=%region_6.7 | all-reduce | flops 128 | bytes 1024 | tf_op jit(solution)/shard_map/psum | solution.py:53
  143.8 1.5 convolution_convert_fusion
  145.3 9.8 %all_to_all.10 = bf16[4,32,1280]{2,1,0:T(8,128)(2,1)} all-to-all(bf16[4,32,1280]{2,1,0:T(8,128)(2,1)S(1)} %bitcast.39), channel_id=1, replica_groups=mesh['group'=2,'attn'=4,'expert'=4] {'expert'}, dimensions={0} | all-to-all | bytes 655360 | tf_op jit(solution)/shard_map/all_to_all | solution.py:74
  155.3 29.8 %all-gather.6.cloned.1.call-done = bf16[128,5120]{1,0:T(8,128)(2,1)} async-done(((bf16[128,1280]{1,0:T(8,128)(2,1)}), bf16[128,5120]{1,0:T(8,128)(2,1)}) %all-gather.6.cloned.1.call-update) | async-done | bytes 1310736 | tf_op jit(solution)/shard_map/all_gather | solution.py:78
  185.2 6.0 %fusion.5 = f32[128,1024]{1,0:T(8,128)S(1)} fusion(bf16[128,5120]{1,0:T(8,128)(2,1)} %all-gather.6.cloned.1.call-done, bf16[1,2,5120,1024]{3,2,1,0:T(8,128)(2,1)} %param.18), kind=kOutput, calls=%fused_computation.5 | convolution fusion | flops 1342177280 | bytes 12320768 | tf_op jit(solution)/shard_map/dot_general | solution.py:79
  191.2 6.3 %fusion.20 = bf16[128,1024]{1,0:T(8,128)(2,1)} fusion(bf16[128,5120]{1,0:T(8,128)(2,1)S(1)} %copy-done.5, bf16[1,2,5120,1024]{3,2,1,0:T(8,128)(2,1)} %param.18, f32[128,1024]{1,0:T(8,128)S(1)} %fusion.5), kind=kOutput, calls=%fused_computation.20 | convolution fusion | flops 1342963712 | bytes 12582912 | tf_op jit(solution)/shard_map/dot_general | solution.py:80
  197.5 27.1 %all-gather.8.cloned.1.call-done = bf16[128,4096]{1,0:T(8,128)(2,1)} async-done(((bf16[128,1024]{1,0:T(8,128)(2,1)}), bf16[128,4096]{1,0:T(8,128)(2,1)}) %all-gather.8.cloned.1.call-update) | async-done | bytes 1048592 | tf_op jit(solution)/shard_map/all_gather | solution.py:83
  224.6 6.7 %fusion.11 = bf16[128,1280]{1,0:T(8,128)(2,1)} fusion(bf16[128,4096]{1,0:T(8,128)(2,1)} %all-gather.8.cloned.1.call-done, bf16[1,4096,1280]{2,1,0:T(8,128)(2,1)} %param.19), kind=kOutput, calls=%fused_computation.12 | convolution fusion | flops 1342341120 | bytes 11862016 | tf_op jit(solution)/shard_map/dot_general | solution.py:82
  231.3 4.1 %all-to-all-start.1 = ((bf16[4,32,1280]{2,1,0:T(8,128)(2,1)}), bf16[4,32,1280]{2,1,0:T(8,128)(2,1)}, u32[]{:S(2)}, u32[]{:S(2)}) async-start(bf16[4,32,1280]{2,1,0:T(8,128)(2,1)} %bitcast.40), calls=%async_computation.2 | async-start | bytes 655360 | tf_op jit(solution)/shard_map/all_to_all | solution.py:87
  235.4 6.8 %all-to-all-done.1 = bf16[4,32,1280]{2,1,0:T(8,128)(2,1)} async-done(((bf16[4,32,1280]{2,1,0:T(8,128)(2,1)}), bf16[4,32,1280]{2,1,0:T(8,128)(2,1)}, u32[]{:S(2)}, u32[]{:S(2)}) %all-to-all-start.1) | async-done | bytes 327712 | tf_op jit(solution)/shard_map/all_to_all | solution.py:87
  242.2 2.3 fusion.10
  (31 shorter events, 2.3 us)
Async XLA Ops:
  6.5 86.1 %copy-start = (bf16[1280,1280]{1,0:T(8,128)(2,1)S(1)}, bf16[1280,1280]{1,0:T(8,128)(2,1)}, u32[]{:S(2)}) copy-start(bf16[1280,1280]{1,0:T(8,128)(2,1)} %param.13) | copy-start | bytes 9830404
  6.5 86.1 %all-gather.4.cloned.1.call-start = ((), (), s32[]{:S(2)}) async-start(), calls=%async_computation.3 | async-start | bytes 1638400 | tf_op jit(solution)/shard_map/all_gather | solution.py:45
  19.6 10.6 %copy-start.4 = (s32[128]{0:T(128)S(1)}, s32[128]{0:T(128)}, u32[]{:S(2)}) copy-start(s32[128]{0:T(128)} %param.12) | copy-start | bytes 1540
  56.3 41.1 %copy-start.2 = (bf16[1280]{0:T(1024)(128)(2,1)S(1)}, bf16[1280]{0:T(1024)(128)(2,1)}, u32[]{:S(2)}) copy-start(bf16[1280]{0:T(1024)(128)(2,1)} %param.15) | copy-start | bytes 7684
  56.3 41.1 %copy-start.3 = (s32[128,1]{0,1:T(1,128)S(1)}, s32[128,1]{0,1:T(1,128)}, u32[]{:S(2)}) copy-start(s32[128,1]{0,1:T(1,128)} %param.17) | copy-start | bytes 1540
  56.3 74.4 %reduce-scatter.2.cloned.1.call-start = ((), (), s32[]{:S(2)}) async-start(), calls=%async_computation.4 | async-start | bytes 3276800 | tf_op jit(solution)/shard_map/reduce_scatter | solution.py:46
  97.4 87.8 %all-gather.6.cloned.1.call-start = ((), (), s32[]{:S(2)}) async-start(), calls=%async_computation.5 | async-start | bytes 1638400 | tf_op jit(solution)/shard_map/all_gather | solution.py:78
  155.1 69.5 %all-gather.8.cloned.1.call-start = ((), (), s32[]{:S(2)}) async-start(), calls=%async_computation.6 | async-start | bytes 1310720 | tf_op jit(solution)/shard_map/all_gather | solution.py:83
  185.2 6.0 %copy-start.5 = (bf16[128,5120]{1,0:T(8,128)(2,1)S(1)}, bf16[128,5120]{1,0:T(8,128)(2,1)}, u32[]{:S(2)}) copy-start(bf16[128,5120]{1,0:T(8,128)(2,1)} %all-gather.6.cloned.1.call-done) | copy-start | bytes 3932164
  197.5 37.9 %copy-start.6 = (f32[128]{0:T(128)S(1)}, f32[128]{0:T(128)}, u32[]{:S(2)}) copy-start(f32[128]{0:T(128)} %param.16) | copy-start | bytes 1540
  224.6 19.9 %copy-start.1 = (bf16[1280,1280]{1,0:T(8,128)(2,1)S(1)}, bf16[1280,1280]{1,0:T(8,128)(2,1)}, u32[]{:S(2)}) copy-start(bf16[1280,1280]{1,0:T(8,128)(2,1)} %param.13) | copy-start | bytes 9830404
  231.3 10.9 %all-to-all-start.1 = ((bf16[4,32,1280]{2,1,0:T(8,128)(2,1)}), bf16[4,32,1280]{2,1,0:T(8,128)(2,1)}, u32[]{:S(2)}, u32[]{:S(2)}) async-start(bf16[4,32,1280]{2,1,0:T(8,128)(2,1)} %bitcast.40), calls=%async_computation.2 | async-start | bytes 655360 | tf_op jit(solution)/shard_map/all_to_all | solution.py:87
Sparse Core Ops, SparseCore 0:
  56.4 36.1 all-gather.3
  97.5 33.1 reduce-scatter.1
  155.2 29.9 all-gather.5
  197.6 26.9 all-gather.7
where the time goes:
time: 252 us; the launch traced here: 251 us
  waiting for transfers between devices  133 us (53%)
  local copies, waits for them, and re-layouts  39.3 us (16%)
  matrix products  37.9 us (15%)
  blocking collectives  21.5 us (9%)
  between operations  13.3 us (5%)
  starting transfers between devices  4.4 us (2%)
    all_gather x1, waiting for transfers between devices, per_device(): gathered = lax.all_gather(heads_out, 'attn', axis=0, tiled=True)  36.2 us
    reduce_scatter x1, waiting for transfers between devices, per_device(): lax.psum_scatter(jnp.dot(gathered, out_weight, preferred_element_type=jnp...  32.8 us
    all_gather x1, waiting for transfers between devices, per_device(): block_piece = lax.all_gather(arrived, 'attn', axis=1, tiled=True)  29.8 us
    all_gather x1, waiting for transfers between devices, per_device(): lax.all_gather(hidden_units, 'attn', axis=1, tiled=True)  27.1 us
    unnamed x17, local copies, waits for them, and re-layouts  15.7 us
    psum x1, blocking collectives, per_device(): total_sq = lax.psum(jnp.sum(hidden_state * hidden_state, axis=1), 'attn')  11.7 us
    all_to_all x1, blocking collectives, per_device(): lax.all_to_all(outgoing.reshape(experts, capacity, -1), 'expert', split_a...  9.81 us
    all_to_all x1, waiting for transfers between devices, per_device(): lax.all_to_all(expert_out.reshape(experts, capacity, -1), 'expert', split...  6.78 us
  transfers between devices with their start and end apart: 5, of which 5 were waited for; matrix products, arithmetic and copies ran while one was open for 0% of the time, Pallas kernels for 0%

commit v1 on v0

v1 whole, which is shorter than its diff:
```python
import functools
import math

import jax
import jax.numpy as jnp
from jax import lax
from jax.experimental import pallas as pl
from jax.experimental.pallas import tpu as pltpu
from jax.sharding import PartitionSpec as P

HD = 128
GROUP_ROWS = 16
MESH = pl.DeviceIdType.MESH
F32 = jnp.float32
BF16 = jnp.bfloat16


def over_tiles(width, body):
    tile = 256 if width % 256 == 0 else width
    if tile == width:
        body(slice(None))
        return

    def step(j, carry):
        body(pl.ds(pl.multiple_of(j * tile, tile), tile))
        return carry

    lax.fori_loop(0, width // tile, step, 0)


class LineGather:
    def __init__(self, buf, send_sem, recv_sem, place, count, subs):
        self.buf, self.send_sem, self.recv_sem = buf, send_sem, recv_sem
        self.place, self.count, self.subs = place, count, subs

    def copy(self, block, sub, way):
        part = self.buf.at[block, sub]
        return pltpu.make_async_remote_copy(
            src_ref=part,
            dst_ref=part,
            send_sem=self.send_sem.at[way, block, sub],
            recv_sem=self.recv_sem.at[block, sub],
            device_id={"attn": self.place + (1 if way == 0 else -1)},
            device_id_type=MESH,
        )

    def can(self, way):
        return self.place < self.count - 1 if way == 0 else self.place > 0

    def forward(self, block, sub, way):
        @pl.when(self.can(way))
        def _():
            self.copy(block, sub, way).start()

    def send_own(self, sub):
        for way in range(2):
            self.forward(self.place, sub, way)

    def arrive(self, step, use):
        for way in range(2):
            block = self.place - step if way == 0 else self.place + step

            @pl.when(block >= 0 if way == 0 else block < self.count)
            def _():
                for sub in range(self.subs):
                    self.copy(block, sub, way).wait_recv()
                    self.forward(block, sub, way)
                use(block)

    def drain(self):
        def step(block, carry):
            for way in range(2):
                mine = block <= self.place if way == 0 else block >= self.place

                @pl.when(jnp.logical_and(self.can(way), mine))
                def _():
                    for sub in range(self.subs):
                        self.copy(block, sub, way).wait_send()

            return carry

        lax.fori_loop(0, self.count, step, 0)


def kernel(
    sizes,
    q_ref,
    kv_hbm,
    len_ref,
    wout_hbm,
    resid_ref,
    gain_ref,
    logit_ref,
    route_col_ref,
    route_row_ref,
    wgu_hbm,
    wd_hbm,
    out_ref,
    kv,
    wout,
    wgu,
    wd,
    ho,
    pbuf,
    mbuf,
    sbuf,
    xbuf,
    hid,
    qbuf,
    obuf,
    fbuf,
    scout,
    scin,
    gacc,
    hbuf,
    dacc,
    ebuf,
    rbuf,
    kv_sem,
    w_sem,
    ho_send,
    ho_recv,
    m_send,
    m_recv,
    x_send,
    x_recv,
    q_send,
    q_recv,
    o_send,
    o_recv,
    f_send,
    f_recv,
    s_send,
    s_recv,
    h_send,
    h_recv,
    r_send,
    r_recv,
):
    n_attn, n_exp = sizes
    n_chip = n_exp // 2
    z = lax.axis_index("attn")
    e = lax.axis_index("expert")
    x, c = e // 2, e % 2
    mate = e + 1 - 2 * c
    rows, q_cols = q_ref.shape
    span = kv.shape[2]
    kv_dev = kv.shape[3] // HD
    group_size = (q_cols // HD) // kv_dev
    moe_rows, cols = resid_ref.shape
    nsub = moe_rows // rows
    ff = wgu.shape[2]
    cap = moe_rows // 4
    slots = n_exp * cap
    ho_subs, h_subs = ho.shape[1], hbuf.shape[1]
    ff_sub = ff // h_subs
    groups = rows // GROUP_ROWS

    def kv_copy(g):
        part = pl.ds(g * GROUP_ROWS, GROUP_ROWS)
        return pltpu.make_async_copy(kv_hbm.at[:, part], kv.at[:, part], kv_sem.at[g])

    for g in range(groups):
        kv_copy(g).start()
    wout_copy = pltpu.make_async_copy(wout_hbm, wout, w_sem.at[0])
    wgu_copy = pltpu.make_async_copy(wgu_hbm.at[0], wgu, w_sem.at[1])
    wd_copy = pltpu.make_async_copy(wd_hbm.at[0], wd, w_sem.at[2])
    wout_copy.start()

    barrier = pltpu.get_barrier_semaphore()
    for d in range(1, n_attn):
        pl.semaphore_signal(
            barrier, inc=1, device_id={"attn": (z + d) % n_attn}, device_id_type=MESH
        )
    for d in range(1, n_exp):
        pl.semaphore_signal(
            barrier, inc=1, device_id={"expert": (e + d) % n_exp}, device_id_type=MESH
        )

    scale = 1.0 / math.sqrt(HD)
    wide = GROUP_ROWS * span
    sub_groups = groups // ho_subs

    def attend(sub, i):
        g = sub * sub_groups + i
        kv_copy(g).wait()
        part = pl.ds(pl.multiple_of(g * GROUP_ROWS, GROUP_ROWS), GROUP_ROWS)
        live = len_ref[part, :]
        first = lax.broadcasted_iota(jnp.int32, (GROUP_ROWS, wide), 0) * span
        slot = lax.broadcasted_iota(jnp.int32, (GROUP_ROWS, wide), 1) - first
        mask = jnp.logical_and(slot >= 0, slot < live)
        for k in range(kv_dev):
            lanes = slice(k * HD, (k + 1) * HD)
            heads = [k * group_size + h for h in range(group_size)]
            stacked = jnp.concatenate([q_ref[part, h * HD : (h + 1) * HD] for h in heads], axis=0)
            keys = kv[0, part, :, lanes].reshape(wide, HD)
            values = kv[1, part, :, lanes].reshape(wide, HD)
            s = lax.dot_general(
                stacked, keys, (((1,), (1,)), ((), ())), preferred_element_type=F32
            ) * scale
            s = jnp.where(mask[None], s.reshape(group_size, GROUP_ROWS, wide), -1e30)
            p = jnp.exp(s - jnp.max(s, axis=-1, keepdims=True))
            p = (p / jnp.sum(p, axis=-1, keepdims=True)).astype(BF16)
            o = jnp.dot(
                p.reshape(group_size * GROUP_ROWS, wide), values, preferred_element_type=F32
            ).astype(BF16)
            to = pl.ds(pl.multiple_of(i * GROUP_ROWS, GROUP_ROWS), GROUP_ROWS)
            for n, h in enumerate(heads):
                ho[z, sub, to, h * HD : (h + 1) * HD] = o[n * GROUP_ROWS : (n + 1) * GROUP_ROWS]

    ho_line = LineGather(ho, ho_send, ho_recv, z, n_attn, ho_subs)
    for sub in range(ho_subs):

        def attend_step(i, carry, sub=sub):
            attend(sub, i)
            return carry

        lax.fori_loop(0, sub_groups, attend_step, 0)
        if sub == 0:
            wgu_copy.start()
            wd_copy.start()
            pl.semaphore_wait(barrier, n_attn - 1 + n_exp - 1)
        ho_line.send_own(sub)

    def mate_copy(b):
        return pltpu.make_async_remote_copy(
            src_ref=pbuf.at[b],
            dst_ref=mbuf.at[b],
            send_sem=m_send.at[b],
            recv_sem=m_recv.at[b],
            device_id={"expert": mate},
            device_id_type=MESH,
        )

    def chip_copy(b):
        return pltpu.make_async_remote_copy(
            src_ref=sbuf.at[b],
            dst_ref=xbuf.at[x, b % nsub],
            send_sem=x_send.at[b],
            recv_sem=x_recv.at[x, b % nsub],
            device_id={"expert": (b // nsub) // 2 * 2 + c},
            device_id_type=MESH,
        )

    def chip_arrival(src, sub):
        return pltpu.make_async_remote_copy(
            src_ref=xbuf.at[src, sub],
            dst_ref=xbuf.at[src, sub],
            send_sem=x_send.at[0],
            recv_sem=x_recv.at[src, sub],
            device_id={"expert": src * 2 + c},
            device_id_type=MESH,
        )

    def project(b):
        block = ho[b].reshape(rows, q_cols)

        def tile(at):
            pbuf[b, :, at] = jnp.dot(block, wout[:, at], preferred_element_type=F32)

        over_tiles(cols, tile)

        @pl.when((b // nsub) % 2 != c)
        def _():
            mate_copy(b).start()

    def combine(b):
        @pl.when((b // nsub) % 2 == c)
        def _():
            mate_copy(b).wait_recv()

            @pl.when((b // nsub) // 2 != x)
            def _():
                sbuf[b] = (pbuf[b] + mbuf[b]).astype(BF16)
                chip_copy(b).start()

    wout_copy.wait()
    project(z)
    combine(z)

    def project_step(t, carry):
        ho_line.arrive(t, project)

        @pl.when(z - t >= 0)
        def _():
            combine(z - t)

        @pl.when(z + t < n_attn)
        def _():
            combine(z + t)

        return carry

    lax.fori_loop(1, n_attn, project_step, 0)

    route_row = route_row_ref[...]
    route_col = route_col_ref[...]
    at0 = lax.broadcasted_iota(jnp.int32, (moe_rows, moe_rows), 0)
    at1 = lax.broadcasted_iota(jnp.int32, (moe_rows, moe_rows), 1)
    same = route_col == route_row
    rank_row = jnp.sum(
        jnp.where(jnp.logical_and(same, at0 < at1), 1.0, 0.0), axis=0, keepdims=True
    ).astype(jnp.int32)
    rank_col = jnp.sum(
        jnp.where(jnp.logical_and(same, at1 < at0), 1.0, 0.0), axis=1, keepdims=True
    ).astype(jnp.int32)
    placed = (route_row * cap + rank_row) == lax.broadcasted_iota(
        jnp.int32, (slots, moe_rows), 0
    )
    placed_t = (route_col * cap + rank_col) == lax.broadcasted_iota(
        jnp.int32, (moe_rows, slots), 1
    )

    square_sum = None
    for sub in range(nsub):
        part = slice(sub * rows, (sub + 1) * rows)
        b = e * nsub + sub
        total = resid_ref[part, :].astype(F32) + (pbuf[b] + mbuf[b])
        for d in range(1, n_chip):
            src = (x + d) % n_chip
            chip_arrival(src, sub).wait_recv()
            total = total + xbuf[src, sub].astype(F32)
        hid[part, :] = total
    hidden = hid[...]
    square_sum = jnp.sum(hidden * hidden, axis=1, keepdims=True)
    square_row = jnp.sum(jnp.where(at0 == at1, square_sum, 0.0), axis=0, keepdims=True)
    qbuf[z] = jnp.broadcast_to(square_row, (8, moe_rows))

    def square_copy(d, src):
        return pltpu.make_async_remote_copy(
            src_ref=qbuf.at[src],
            dst_ref=qbuf.at[src],
            send_sem=q_send.at[d],
            recv_sem=q_recv.at[src],
            device_id={"attn": (z + d) % n_attn},
            device_id_type=MESH,
        )

    for d in range(1, n_attn):
        square_copy(d, z).start()

    scaled = (hidden * gain_ref[...].astype(F32)).astype(BF16)
    one_hot = jnp.where(placed, 1.0, 0.0).astype(BF16)
    obuf[...] = (
        jnp.dot(one_hot, scaled, preferred_element_type=F32).astype(BF16).reshape(n_exp, cap, cols)
    )

    def peer(d):
        to = (e + d) % n_exp
        return to, to // 2, to % 2

    def spread(src, dst, send_sem, recv_sem, to):
        return pltpu.make_async_remote_copy(
            src_ref=src,
            dst_ref=dst,
            send_sem=send_sem,
            recv_sem=recv_sem,
            device_id={"expert": to},
            device_id_type=MESH,
        )

    def dispatch_copy(d):
        to, to_x, _ = peer(d)
        rel = (x - to_x + n_chip) % n_chip
        return spread(
            obuf.at[to], fbuf.at[z, rel, c], o_send.at[d], o_recv.at[rel, c], to
        )

    def scale_copy(d):
        to, to_x, _ = peer(d)
        rel = (x - to_x + n_chip) % n_chip
        return spread(
            scout.at[to], scin.at[rel, c], s_send.at[d], s_recv.at[rel, c], to
        )

    def arrival(dst, sem):
        return spread(dst, dst, o_send.at[0], sem, mate)

    for d in range(1, n_exp):
        dispatch_copy(d).start()
    fbuf[z, 0, c] = obuf[e]
    f_line = LineGather(fbuf, f_send, f_recv, z, n_attn, n_chip)
    for rel in range(n_chip):
        if rel == 0:
            arrival(fbuf.at[z, 0, 1 - c], o_recv.at[0, 1 - c]).wait_recv()
        else:
            for core in range(2):
                arrival(fbuf.at[z, rel, core], o_recv.at[rel, core]).wait_recv()
        f_line.send_own(rel)

    wgu_copy.wait()
    gacc[...] = jnp.zeros_like(gacc)

    def expand(b):
        block = fbuf[b].reshape(slots, cols)
        depth = pl.ds(pl.multiple_of(b * cols, cols), cols)

        def tile(at):
            for i in range(2):
                gacc[i, :, at] += jnp.dot(block, wgu[i, depth, at], preferred_element_type=F32)

        over_tiles(ff, tile)

    expand(z)

    for d in range(1, n_attn):
        square_copy(0, (z + d) % n_attn).wait_recv()
    total_row = qbuf[0][:1]
    for a in range(1, n_attn):
        total_row = total_row + qbuf[a][:1]
    factor_row = lax.rsqrt(total_row / (cols * n_attn) + 1e-05)
    factor = jnp.sum(jnp.where(placed, factor_row, 0.0), axis=1, keepdims=True)
    scout[...] = jnp.broadcast_to(factor, (slots, HD)).reshape(n_exp, cap, HD)
    for d in range(1, n_exp):
        scale_copy(d).start()
    scin[0, c] = scout[e]

    def expand_step(t, carry):
        f_line.arrive(t, expand)
        return carry

    lax.fori_loop(1, n_attn, expand_step, 0)

    arrival(scin.at[0, 1 - c], s_recv.at[0, 1 - c]).wait_recv()
    for rel in range(1, n_chip):
        for core in range(2):
            arrival(scin.at[rel, core], s_recv.at[rel, core]).wait_recv()
    norm = scin[...].reshape(slots, HD)[:, :1]

    h_line = LineGather(hbuf, h_send, h_recv, z, n_attn, h_subs)
    for sub in range(h_subs):
        at = slice(sub * ff_sub, (sub + 1) * ff_sub)
        gate = gacc[0, :, at] * norm
        up = gacc[1, :, at] * norm
        hbuf[z, sub] = (gate / (1.0 + jnp.exp(-gate)) * up).astype(BF16)
        h_line.send_own(sub)

    wd_copy.wait()
    dacc[...] = jnp.zeros_like(dacc)

    def contract(b):
        def tile(at):
            total = dacc[:, at]
            for sub in range(h_subs):
                depth = pl.ds(pl.multiple_of(b * ff + sub * ff_sub, ff_sub), ff_sub)
                total = total + jnp.dot(hbuf[b, sub], wd[depth, at], preferred_element_type=F32)
            dacc[:, at] = total

        over_tiles(cols, tile)

    contract(z)

    def contract_step(t, carry):
        h_line.arrive(t, contract)
        return carry

    lax.fori_loop(1, n_attn, contract_step, 0)

    ebuf[...] = dacc[...].astype(BF16).reshape(n_chip, 2, cap, cols)

    def return_copy(d):
        to, to_x, to_c = peer(d)
        rel = (to_x - x + n_chip) % n_chip
        return spread(ebuf.at[rel, to_c], rbuf.at[e], r_send.at[d], r_recv.at[e], to)

    for d in range(1, n_exp):
        return_copy(d).start()
    rbuf[e] = ebuf[0, c]
    for d in range(1, n_exp):
        src = (e + d) % n_exp
        arrival(rbuf.at[src], r_recv.at[src]).wait_recv()
    one_hot_t = jnp.where(placed_t, 1.0, 0.0).astype(BF16)
    mixing = 1.0 / (1.0 + jnp.exp(-logit_ref[...]))
    combined = jnp.dot(one_hot_t, rbuf[...].reshape(slots, cols), preferred_element_type=F32)
    out_ref[...] = (hid[...] + mixing * combined).astype(BF16)

    ho_line.drain()
    f_line.drain()
    h_line.drain()

    def sums_left(b, carry):
        @pl.when((b // nsub) % 2 != c)
        def _():
            mate_copy(b).wait_send()

        @pl.when(jnp.logical_and((b // nsub) % 2 == c, (b // nsub) // 2 != x))
        def _():
            chip_copy(b).wait_send()

        return carry

    lax.fori_loop(0, n_attn, sums_left, 0)
    for d in range(1, n_attn):
        square_copy(d, z).wait_send()
    for d in range(1, n_exp):
        dispatch_copy(d).wait_send()
        scale_copy(d).wait_send()
        return_copy(d).wait_send()


def per_device(
    queries,
    kv_cache,
    lengths,
    out_weight,
    residual,
    norm_gain,
    route_logit,
    routes,
    w_gate_up,
    w_down,
):
    n_attn, n_exp = lax.axis_size("attn"), lax.axis_size("expert")
    n_chip = n_exp // 2
    rows, q_cols = queries.shape
    moe_rows, cols = residual.shape
    nsub = moe_rows // rows
    cap = moe_rows // 4
    slots = n_exp * cap
    ff = w_gate_up.shape[3]
    ho_subs, h_subs = 2, 2
    vmem = pl.BlockSpec(memory_space=pltpu.VMEM)
    hbm = pl.BlockSpec(memory_space=pl.ANY)
    dma = pltpu.SemaphoreType.DMA
    return pl.pallas_call(
        functools.partial(kernel, (n_attn, n_exp)),
        out_shape=jax.ShapeDtypeStruct((moe_rows, cols), BF16),
        in_specs=[vmem, hbm, vmem, hbm, vmem, vmem, vmem, vmem, vmem, hbm, hbm],
        out_specs=vmem,
        scratch_shapes=[
            pltpu.VMEM(kv_cache.shape, BF16),
            pltpu.VMEM(out_weight.shape, BF16),
            pltpu.VMEM(w_gate_up.shape[1:], BF16),
            pltpu.VMEM(w_down.shape[1:], BF16),
            pltpu.VMEM((n_attn, ho_subs, rows // ho_subs, q_cols), BF16),
            pltpu.VMEM((n_attn, rows, cols), F32),
            pltpu.VMEM((n_attn, rows, cols), F32),
            pltpu.VMEM((n_attn, rows, cols), BF16),
            pltpu.VMEM((n_chip, nsub, rows, cols), BF16),
            pltpu.VMEM((moe_rows, cols), F32),
            pltpu.VMEM((n_attn, 8, moe_rows), F32),
            pltpu.VMEM((n_exp, cap, cols), BF16),
            pltpu.VMEM((n_attn, n_chip, 2, cap, cols), BF16),
            pltpu.VMEM((n_exp, cap, HD), F32),
            pltpu.VMEM((n_chip, 2, cap, HD), F32),
            pltpu.VMEM((2, slots, ff), F32),
            pltpu.VMEM((n_attn, h_subs, slots, ff // h_subs), BF16),
            pltpu.VMEM((slots, cols), F32),
            pltpu.VMEM((n_chip, 2, cap, cols), BF16),
            pltpu.VMEM((n_exp, cap, cols), BF16),
            dma((rows // GROUP_ROWS,)),
            dma((3,)),
            dma((2, n_attn, ho_subs)),
            dma((n_attn, ho_subs)),
            dma((n_attn,)),
            dma((n_attn,)),
            dma((n_attn,)),
            dma((n_chip, nsub)),
            dma((n_attn,)),
            dma((n_attn,)),
            dma((n_exp,)),
            dma((n_chip, 2)),
            dma((2, n_attn, n_chip)),
            dma((n_attn, n_chip)),
            dma((n_exp,)),
            dma((n_chip, 2)),
            dma((2, n_attn, h_subs)),
            dma((n_attn, h_subs)),
            dma((n_exp,)),
            dma((n_exp,)),
        ],
        compiler_params=pltpu.CompilerParams(
            collective_id=0, has_side_effects=True, vmem_limit_bytes=63 * 1024 * 1024
        ),
    )(
        queries,
        kv_cache,
        lengths.reshape(rows, 1),
        out_weight,
        residual,
        norm_gain.reshape(1, cols),
        route_logit.reshape(moe_rows, 1),
        routes,
        routes.reshape(1, moe_rows),
        w_gate_up,
        w_down,
    )


def solution(mesh):
    return jax.shard_map(
        per_device,
        mesh=mesh,
        in_specs=(
            P(("group", "attn"), "expert"),
            P(None, ("group", "attn"), None, "expert"),
            P(("group", "attn")),
            P("expert", "attn"),
            P(("group", "expert"), "attn"),
            P("attn"),
            P(("group", "expert")),
            P(("group", "expert"), None),
            P("expert", None, None, "attn"),
            P("expert", None, "attn"),
        ),
        out_specs=P(("group", "expert"), "attn"),
        check_vma=False,
    )
```

time: 252 us -> 105 us (0.42)
  waiting for transfers between devices: 133 us -> 0 us
  Pallas kernels: 0 us -> 97.6 us
  matrix products: 37.9 us -> 0 us
  local copies, waits for them, and re-layouts: 39.3 us -> 7.15 us
  blocking collectives: 21.5 us -> 0 us
  between operations: 13.3 us -> 0.01 us
  starting transfers between devices: 4.4 us -> 0 us
    pallas_call x0 -> x1, Pallas kernels: none -> 97.6 us  [per_device(): pl.pallas_call(functools.partial(kernel, (n_attn, n_exp)), out_shape=jax....]
    all_gather x3 -> x0, waiting for transfers between devices: 93.1 us -> none  [the longest x1 36.2 us: per_device(): gathered = lax.all_gather(heads_out, 'attn', axis=0, tiled=True)]
    reduce_scatter x1 -> x0, waiting for transfers between devices: 32.8 us -> none  [per_device(): lax.psum_scatter(jnp.dot(gathered, out_weight, preferred_element_type=jnp...]
    dot_general x7 -> x0, matrix products: 32 us -> none  [the longest x1 6.7 us: per_device(): jnp.dot(lax.all_gather(hidden_units, 'attn', axis=1, tiled=True), down_w,...]
    another operation x2 -> x0, local copies, waits for them, and re-layouts: 13.1 us -> none  [the longest x1 6.57 us: per_device(): value_heads = kv_cache[1].reshape(rows_dev, cache_span, kv_dev, HD)]
    unnamed x17 -> x2, local copies, waits for them, and re-layouts: 15.7 us -> 3.1 us
    psum x1 -> x0, blocking collectives: 11.7 us -> none  [per_device(): total_sq = lax.psum(jnp.sum(hidden_state * hidden_state, axis=1), 'attn')]
    all_to_all x1 -> x0, blocking collectives: 9.81 us -> none  [per_device(): lax.all_to_all(outgoing.reshape(experts, capacity, -1), 'expert', split_a...]
  transfers between devices with their start and end apart: 5 -> 0, of which waited for: 5 -> 0; matrix products, arithmetic and copies ran while one was open for 0% -> 0% of each run, Pallas kernels for 0% -> 0%
where the time goes in v1:
time: 105 us
  Pallas kernels  97.6 us (93%)
  local copies, waits for them, and re-layouts  7.15 us (7%)
    pallas_call x1, Pallas kernels, per_device(): pl.pallas_call(functools.partial(kernel, (n_attn, n_exp)), out_shape=jax....  97.6 us
    unnamed x2, local copies, waits for them, and re-layouts  3.1 us

profile of v1, /device:TPU:0, one launch (start us, length us, event | category | flops | bytes accessed | tf_op | source)
XLA Modules:
  0.0 104.7 jit_solution(16246986638847121595)
XLA Ops:
  0.0 1.3 %reshape.13.gain_ref = bf16[1,1280]{1,0:T(2,128)(2,1)} reshape(bf16[1280]{0:T(1024)(128)(2,1)} %param.15) | data formatting | bytes 5120 | tf_op jit(solution)/shard_map/reshape | solution.py:581
  1.3 1.4 %copy.11.len_ref = s32[128,1]{1,0:T(8,128)} copy(s32[128,1]{0,1:T(1,128)} %bitcast.4) | data formatting | bytes 1024 | tf_op jit(solution)/shard_map/reshape | solution.py:578
  2.7 1.4 %copy.12.logit_ref = f32[128,1]{1,0:T(8,128)} copy(f32[128,1]{0,1:T(1,128)} %bitcast.5) | data formatting | bytes 1024 | tf_op jit(solution)/shard_map/reshape | solution.py:582
  4.1 1.4 %copy.13.route_col_ref = s32[128,1]{1,0:T(8,128)} copy(s32[128,1]{0,1:T(1,128)} %param.17) | data formatting | bytes 1024 | tf_op args[7]
  5.4 97.6 %shard_map.100 = bf16[128,1280]{1,0:T(8,128)(2,1)} custom-call(bf16[128,1280]{1,0:T(8,128)(2,1)} %q_ref.1, bf16[2,128,64,256]{3,2,1,0:T(8,128)(2,1)} %kv_hbm.1, s32[128,1]{1,0:T(8,128)} %copy.11.len_ref, bf16[1280,1280]{1,0:T(8,128)(2,1)} %wout_hbm.1, bf16[128,1280]{1,0:T(8,128)(2,1)} %resid_ref.1, bf16[1,1280]{1,0:T(2,128)(2,1)} %reshape.13.gain_ref, ...), custom_call_target="tpu_custom_call" | custom-call | tf_op jit(solution)/shard_map/pallas_call | solution.py:525
  103.0 1.7 %copy.15 = bf16[128,1280]{1,0:T(8,128)(2,1)} copy(bf16[128,1280]{1,0:T(8,128)(2,1)} %shard_map.100) | data formatting | bytes 655360

commit v2 on v1

--- a/solution.py
+++ b/solution.py
@@ -56,16 +56,26 @@
         for way in range(2):
             self.forward(self.place, sub, way)
 
-    def arrive(self, step, use):
-        for way in range(2):
-            block = self.place - step if way == 0 else self.place + step
-
-            @pl.when(block >= 0 if way == 0 else block < self.count)
-            def _():
-                for sub in range(self.subs):
-                    self.copy(block, sub, way).wait_recv()
-                    self.forward(block, sub, way)
-                use(block)
+    def arrive(self, step, use=None, use_part=None):
+        def of_ways(act):
+            for way in range(2):
+                block = self.place - step if way == 0 else self.place + step
+
+                @pl.when(block >= 0 if way == 0 else block < self.count)
+                def _():
+                    act(block, way)
+
+        for sub in range(self.subs):
+
+            def take(block, way, sub=sub):
+                self.copy(block, sub, way).wait_recv()
+                self.forward(block, sub, way)
+
+            of_ways(take)
+            if use_part is not None:
+                of_ways(lambda block, way, sub=sub: use_part(block, sub))
+        if use is not None:
+            of_ways(lambda block, way: use(block))
 
     def drain(self):
         def step(block, carry):
@@ -91,7 +101,6 @@
     resid_ref,
     gain_ref,
     logit_ref,
-    route_col_ref,
     route_row_ref,
     wgu_hbm,
     wd_hbm,
@@ -116,6 +125,7 @@
     dacc,
     ebuf,
     rbuf,
+    live_col,
     kv_sem,
     w_sem,
     ho_send,
@@ -177,6 +187,15 @@
             barrier, inc=1, device_id={"expert": (e + d) % n_exp}, device_id_type=MESH
         )
 
+    def column(row):
+        side = row.shape[1]
+        diagonal = lax.broadcasted_iota(jnp.int32, (side, side), 0) == lax.broadcasted_iota(
+            jnp.int32, (side, side), 1
+        )
+        return jnp.sum(jnp.where(diagonal, row, 0.0), axis=1, keepdims=True)
+
+    live_col[...] = jnp.broadcast_to(column(len_ref[...].astype(F32)), live_col.shape)
+
     scale = 1.0 / math.sqrt(HD)
     wide = GROUP_ROWS * span
     sub_groups = groups // ho_subs
@@ -185,7 +204,7 @@
         g = sub * sub_groups + i
         kv_copy(g).wait()
         part = pl.ds(pl.multiple_of(g * GROUP_ROWS, GROUP_ROWS), GROUP_ROWS)
-        live = len_ref[part, :]
+        live = live_col[part, :][:, :1].astype(jnp.int32)
         first = lax.broadcasted_iota(jnp.int32, (GROUP_ROWS, wide), 0) * span
         slot = lax.broadcasted_iota(jnp.int32, (GROUP_ROWS, wide), 1) - first
         mask = jnp.logical_and(slot >= 0, slot < live)
@@ -294,7 +313,7 @@
     lax.fori_loop(1, n_attn, project_step, 0)
 
     route_row = route_row_ref[...]
-    route_col = route_col_ref[...]
+    route_col = column(route_row.astype(F32)).astype(jnp.int32)
     at0 = lax.broadcasted_iota(jnp.int32, (moe_rows, moe_rows), 0)
     at1 = lax.broadcasted_iota(jnp.int32, (moe_rows, moe_rows), 1)
     same = route_col == route_row
@@ -438,20 +457,19 @@
     wd_copy.wait()
     dacc[...] = jnp.zeros_like(dacc)
 
-    def contract(b):
+    def contract(b, sub):
+        depth = pl.ds(pl.multiple_of(b * ff + sub * ff_sub, ff_sub), ff_sub)
+
         def tile(at):
-            total = dacc[:, at]
-            for sub in range(h_subs):
-                depth = pl.ds(pl.multiple_of(b * ff + sub * ff_sub, ff_sub), ff_sub)
-                total = total + jnp.dot(hbuf[b, sub], wd[depth, at], preferred_element_type=F32)
-            dacc[:, at] = total
+            dacc[:, at] += jnp.dot(hbuf[b, sub], wd[depth, at], preferred_element_type=F32)
 
         over_tiles(cols, tile)
 
-    contract(z)
+    for sub in range(h_subs):
+        contract(z, sub)
 
     def contract_step(t, carry):
-        h_line.arrive(t, contract)
+        h_line.arrive(t, use_part=contract)
         return carry
 
     lax.fori_loop(1, n_attn, contract_step, 0)
@@ -470,7 +488,7 @@
         src = (e + d) % n_exp
         arrival(rbuf.at[src], r_recv.at[src]).wait_recv()
     one_hot_t = jnp.where(placed_t, 1.0, 0.0).astype(BF16)
-    mixing = 1.0 / (1.0 + jnp.exp(-logit_ref[...]))
+    mixing = 1.0 / (1.0 + jnp.exp(-column(logit_ref[...])))
     combined = jnp.dot(one_hot_t, rbuf[...].reshape(slots, cols), preferred_element_type=F32)
     out_ref[...] = (hid[...] + mixing * combined).astype(BF16)
 
@@ -518,14 +536,14 @@
     cap = moe_rows // 4
     slots = n_exp * cap
     ff = w_gate_up.shape[3]
-    ho_subs, h_subs = 2, 2
+    ho_subs, h_subs = 4, max(1, min(4, ff // 256))
     vmem = pl.BlockSpec(memory_space=pltpu.VMEM)
     hbm = pl.BlockSpec(memory_space=pl.ANY)
     dma = pltpu.SemaphoreType.DMA
     return pl.pallas_call(
         functools.partial(kernel, (n_attn, n_exp)),
         out_shape=jax.ShapeDtypeStruct((moe_rows, cols), BF16),
-        in_specs=[vmem, hbm, vmem, hbm, vmem, vmem, vmem, vmem, vmem, hbm, hbm],
+        in_specs=[vmem, hbm, vmem, hbm, vmem, vmem, vmem, vmem, hbm, hbm],
         out_specs=vmem,
         scratch_shapes=[
             pltpu.VMEM(kv_cache.shape, BF16),
@@ -548,6 +566,7 @@
             pltpu.VMEM((slots, cols), F32),
             pltpu.VMEM((n_chip, 2, cap, cols), BF16),
             pltpu.VMEM((n_exp, cap, cols), BF16),
+            pltpu.VMEM((rows, HD), F32),
             dma((rows // GROUP_ROWS,)),
             dma((3,)),
             dma((2, n_attn, ho_subs)),
@@ -575,12 +594,11 @@
     )(
         queries,
         kv_cache,
-        lengths.reshape(rows, 1),
+        lengths.reshape(1, rows),
         out_weight,
         residual,
         norm_gain.reshape(1, cols),
-        route_logit.reshape(moe_rows, 1),
-        routes,
+        route_logit.reshape(1, moe_rows),
         routes.reshape(1, moe_rows),
         w_gate_up,
         w_down,

time: 105 us -> 91.8 us (0.87)
  Pallas kernels: 97.6 us -> 88.3 us
  local copies, waits for them, and re-layouts: 7.15 us -> 3 us
    pallas_call x1, Pallas kernels: 97.6 us -> 88.3 us  [per_device(): pl.pallas_call(functools.partial(kernel, (n_attn, n_exp)), out_shape=jax....]
    reshape x2 -> x0, local copies, waits for them, and re-layouts: 2.78 us -> none  [the longest x1 1.39 us: per_device(): lengths.reshape(rows, 1)]
    unnamed x2 -> x1, local copies, waits for them, and re-layouts: 3.1 us -> 1.72 us
where the time goes in v2:
time: 91.8 us; the launch traced here: 91.3 us
  Pallas kernels  88.3 us (96%)
  local copies, waits for them, and re-layouts  3 us (3%)
    pallas_call x1, Pallas kernels, per_device(): pl.pallas_call(functools.partial(kernel, (n_attn, n_exp)), out_shape=jax....  88.3 us

profile of v2, /device:TPU:0, one launch (start us, length us, event | category | flops | bytes accessed | tf_op | source)
XLA Modules:
  0.0 91.3 jit_solution(2242640895067255380)
XLA Ops:
  0.0 1.3 %reshape.13.gain_ref = bf16[1,1280]{1,0:T(2,128)(2,1)} reshape(bf16[1280]{0:T(1024)(128)(2,1)} %param.15) | data formatting | bytes 5120 | tf_op jit(solution)/shard_map/reshape | solution.py:600
  1.3 88.3 %shard_map.100 = bf16[128,1280]{1,0:T(8,128)(2,1)} custom-call(bf16[128,1280]{1,0:T(8,128)(2,1)} %q_ref.1, bf16[2,128,64,256]{3,2,1,0:T(8,128)(2,1)} %kv_hbm.1, s32[1,128]{1,0:T(1,128)} %bitcast.3, bf16[1280,1280]{1,0:T(8,128)(2,1)} %wout_hbm.1, bf16[128,1280]{1,0:T(8,128)(2,1)} %resid_ref.1, bf16[1,1280]{1,0:T(2,128)(2,1)} %reshape.13.gain_ref, ...), custom_call_target="tpu_custom_call" | custom-call | tf_op jit(solution)/shard_map/pallas_call | solution.py:543
  89.6 1.7 %copy.12 = bf16[128,1280]{1,0:T(8,128)(2,1)} copy(bf16[128,1280]{1,0:T(8,128)(2,1)} %shard_map.100) | data formatting | bytes 655360

commit v3 on v2

--- a/solution.py
+++ b/solution.py
@@ -165,6 +165,7 @@
     ho_subs, h_subs = ho.shape[1], hbuf.shape[1]
     ff_sub = ff // h_subs
     groups = rows // GROUP_ROWS
+    halves, width = pbuf.shape[1], pbuf.shape[3]
 
     def kv_copy(g):
         part = pl.ds(g * GROUP_ROWS, GROUP_ROWS)
@@ -241,57 +242,56 @@
             pl.semaphore_wait(barrier, n_attn - 1 + n_exp - 1)
         ho_line.send_own(sub)
 
-    def mate_copy(b):
+    def mate_copy(b, half):
         return pltpu.make_async_remote_copy(
-            src_ref=pbuf.at[b],
-            dst_ref=mbuf.at[b],
-            send_sem=m_send.at[b],
-            recv_sem=m_recv.at[b],
+            src_ref=pbuf.at[b, half],
+            dst_ref=mbuf.at[b, half],
+            send_sem=m_send.at[b, half],
+            recv_sem=m_recv.at[b, half],
             device_id={"expert": mate},
             device_id_type=MESH,
         )
 
-    def chip_copy(b):
+    def chip_copy(b, half):
         return pltpu.make_async_remote_copy(
-            src_ref=sbuf.at[b],
-            dst_ref=xbuf.at[x, b % nsub],
-            send_sem=x_send.at[b],
-            recv_sem=x_recv.at[x, b % nsub],
+            src_ref=sbuf.at[b, half],
+            dst_ref=xbuf.at[x, b % nsub, half],
+            send_sem=x_send.at[b, half],
+            recv_sem=x_recv.at[x, b % nsub, half],
             device_id={"expert": (b // nsub) // 2 * 2 + c},
             device_id_type=MESH,
         )
 
-    def chip_arrival(src, sub):
+    def chip_arrival(src, sub, half):
         return pltpu.make_async_remote_copy(
-            src_ref=xbuf.at[src, sub],
-            dst_ref=xbuf.at[src, sub],
-            send_sem=x_send.at[0],
-            recv_sem=x_recv.at[src, sub],
+            src_ref=xbuf.at[src, sub, half],
+            dst_ref=xbuf.at[src, sub, half],
+            send_sem=x_send.at[0, 0],
+            recv_sem=x_recv.at[src, sub, half],
             device_id={"expert": src * 2 + c},
             device_id_type=MESH,
         )
 
     def project(b):
         block = ho[b].reshape(rows, q_cols)
-
-        def tile(at):
-            pbuf[b, :, at] = jnp.dot(block, wout[:, at], preferred_element_type=F32)
-
-        over_tiles(cols, tile)
-
-        @pl.when((b // nsub) % 2 != c)
-        def _():
-            mate_copy(b).start()
+        for half in range(halves):
+            at = slice(half * width, (half + 1) * width)
+            pbuf[b, half] = jnp.dot(block, wout[:, at], preferred_element_type=F32)
+
+            @pl.when((b // nsub) % 2 != c)
+            def _():
+                mate_copy(b, half).start()
 
     def combine(b):
         @pl.when((b // nsub) % 2 == c)
         def _():
-            mate_copy(b).wait_recv()
-
-            @pl.when((b // nsub) // 2 != x)
-            def _():
-                sbuf[b] = (pbuf[b] + mbuf[b]).astype(BF16)
-                chip_copy(b).start()
+            for half in range(halves):
+                mate_copy(b, half).wait_recv()
+
+                @pl.when((b // nsub) // 2 != x)
+                def _():
+                    sbuf[b, half] = (pbuf[b, half] + mbuf[b, half]).astype(BF16)
+                    chip_copy(b, half).start()
 
     wout_copy.wait()
     project(z)
@@ -334,12 +334,14 @@
     for sub in range(nsub):
         part = slice(sub * rows, (sub + 1) * rows)
         b = e * nsub + sub
-        total = resid_ref[part, :].astype(F32) + (pbuf[b] + mbuf[b])
-        for d in range(1, n_chip):
-            src = (x + d) % n_chip
-            chip_arrival(src, sub).wait_recv()
-            total = total + xbuf[src, sub].astype(F32)
-        hid[part, :] = total
+        for half in range(halves):
+            at = slice(half * width, (half + 1) * width)
+            total = resid_ref[part, at].astype(F32) + (pbuf[b, half] + mbuf[b, half])
+            for d in range(1, n_chip):
+                src = (x + d) % n_chip
+                chip_arrival(src, sub, half).wait_recv()
+                total = total + xbuf[src, sub, half].astype(F32)
+            hid[part, at] = total
     hidden = hid[...]
     square_sum = jnp.sum(hidden * hidden, axis=1, keepdims=True)
     square_row = jnp.sum(jnp.where(at0 == at1, square_sum, 0.0), axis=0, keepdims=True)
@@ -499,11 +501,13 @@
     def sums_left(b, carry):
         @pl.when((b // nsub) % 2 != c)
         def _():
-            mate_copy(b).wait_send()
+            for half in range(halves):
+                mate_copy(b, half).wait_send()
 
         @pl.when(jnp.logical_and((b // nsub) % 2 == c, (b // nsub) // 2 != x))
         def _():
-            chip_copy(b).wait_send()
+            for half in range(halves):
+                chip_copy(b, half).wait_send()
 
         return carry
 
@@ -536,6 +540,8 @@
     cap = moe_rows // 4
     slots = n_exp * cap
     ff = w_gate_up.shape[3]
+    halves = 2 if cols % (2 * HD) == 0 else 1
+    width = cols // halves
     ho_subs, h_subs = 4, max(1, min(4, ff // 256))
     vmem = pl.BlockSpec(memory_space=pltpu.VMEM)
     hbm = pl.BlockSpec(memory_space=pl.ANY)
@@ -551,10 +557,10 @@
             pltpu.VMEM(w_gate_up.shape[1:], BF16),
             pltpu.VMEM(w_down.shape[1:], BF16),
             pltpu.VMEM((n_attn, ho_subs, rows // ho_subs, q_cols), BF16),
-            pltpu.VMEM((n_attn, rows, cols), F32),
-            pltpu.VMEM((n_attn, rows, cols), F32),
-            pltpu.VMEM((n_attn, rows, cols), BF16),
-            pltpu.VMEM((n_chip, nsub, rows, cols), BF16),
+            pltpu.VMEM((n_attn, halves, rows, width), F32),
+            pltpu.VMEM((n_attn, halves, rows, width), F32),
+            pltpu.VMEM((n_attn, halves, rows, width), BF16),
+            pltpu.VMEM((n_chip, nsub, halves, rows, width), BF16),
             pltpu.VMEM((moe_rows, cols), F32),
             pltpu.VMEM((n_attn, 8, moe_rows), F32),
             pltpu.VMEM((n_exp, cap, cols), BF16),
@@ -571,10 +577,10 @@
             dma((3,)),
             dma((2, n_attn, ho_subs)),
             dma((n_attn, ho_subs)),
-            dma((n_attn,)),
-            dma((n_attn,)),
-            dma((n_attn,)),
-            dma((n_chip, nsub)),
+            dma((n_attn, halves)),
+            dma((n_attn, halves)),
+            dma((n_attn, halves)),
+            dma((n_chip, nsub, halves)),
             dma((n_attn,)),
             dma((n_attn,)),
             dma((n_exp,)),

time: 91.8 us -> 90.5 us (0.986)
  Pallas kernels: 88.3 us -> 87 us
    pallas_call x1, Pallas kernels: 88.3 us -> 87 us  [per_device(): pl.pallas_call(functools.partial(kernel, (n_attn, n_exp)), out_shape=jax....]
where the time goes in v3:
time: 90.5 us; the launch traced here: 90 us
  Pallas kernels  87 us (96%)
  local copies, waits for them, and re-layouts  3 us (3%)
    pallas_call x1, Pallas kernels, per_device(): pl.pallas_call(functools.partial(kernel, (n_attn, n_exp)), out_shape=jax....  87 us

profile of v3, /device:TPU:0, one launch (start us, length us, event | category | flops | bytes accessed | tf_op | source)
XLA Modules:
  0.0 90.0 jit_solution(12945478566274370054)
XLA Ops:
  0.0 1.3 %reshape.13.gain_ref = bf16[1,1280]{1,0:T(2,128)(2,1)} reshape(bf16[1280]{0:T(1024)(128)(2,1)} %param.15) | data formatting | bytes 5120 | tf_op jit(solution)/shard_map/reshape | solution.py:606
  1.3 87.0 %shard_map.100 = bf16[128,1280]{1,0:T(8,128)(2,1)} custom-call(bf16[128,1280]{1,0:T(8,128)(2,1)} %q_ref.1, bf16[2,128,64,256]{3,2,1,0:T(8,128)(2,1)} %kv_hbm.1, s32[1,128]{1,0:T(1,128)} %bitcast.3, bf16[1280,1280]{1,0:T(8,128)(2,1)} %wout_hbm.1, bf16[128,1280]{1,0:T(8,128)(2,1)} %resid_ref.1, bf16[1,1280]{1,0:T(2,128)(2,1)} %reshape.13.gain_ref, ...), custom_call_target="tpu_custom_call" | custom-call | tf_op jit(solution)/shard_map/pallas_call | solution.py:549
  88.3 1.7 %copy.12 = bf16[128,1280]{1,0:T(8,128)(2,1)} copy(bf16[128,1280]{1,0:T(8,128)(2,1)} %shard_map.100) | data formatting | bytes 655360
